TPU v7x, 256 devices: a whole 4x4x8 slice. The times are simulated.
256 devices in a mesh: region: 64 (over z, y, core), sub: 4 (over x).
Axes of the slice: x: 4, y: 4, z: 8, core: 2. Of those that a mesh axis runs over, the one named last changes fastest.
Arguments:
- innovations: float32 [4096, 16, 128], P(('region', 'sub'))
- ensemble: float32 [4096, 64, 128], P(('region', 'sub')), may hold values from -3 to 3
- coords: int32 [4096, 2, 128], P(('region', 'sub')), may hold values from 0 to 255, as said below
- obs_error: float32 [4096, 128], P(('region', 'sub')), may hold values from 2.5 to 5
- pair_cols: int32 [4096, 9], P(('region', 'sub')), may hold values from 0 to 4095, as said below
- pair_count: int32 [4096], P(('region', 'sub')), may hold values from 1 to 9, as said below
Outputs:
- analysis_weights: float32 [4096, 16, 128], P(('region', 'sub'))
- residual: float32 [4096, 16, 128], P(('region', 'sub'))
Inputs may be any that keep to these rules, and one draw needn't show every extreme that they name: `coords`: the first coordinate lies in 0 to 63, the second in 0 to 255. `pair_cols`: the first pair_count[b] entries of row b list, in ascending order, the blocks paired with block b: always b itself, and only blocks c with |c - b| <= 4; c lists b exactly when b lists c. The remaining slots hold b. `pair_count`: the largest value 9 is taken in every draw.
All inputs are finite; a program needn't handle non-finite values.
Results may differ from a plain program's by a relative error of at most 0.00045.
Values sent between devices are 32-bit elements; how exact they have to be, the bound alone decides.
A program may use at most 64 MiB of HBM per device.

v0:
```python
import jax
import jax.numpy as jnp
from jax import lax
from jax.experimental import pallas as pl
from jax.experimental.pallas import tpu as pltpu
from jax.sharding import PartitionSpec as P

MESH = pl.DeviceIdType.MESH
F32 = jnp.float32
BF16 = jnp.bfloat16

LIMIT = 40 * 1024 * 1024
EARLY = 2
NB = 16
W = 4
NX = NB + 2 * W
SLOTS = 2 * W + 1
HALF = W + 1
OBS = 128
RHS = 16
MEM = 64

STATIC_VAR = 0.002
LOG2E = 1.4426950408889634
C_CORR = -LOG2E / 150.0
C_LOC = -LOG2E / (2.0 * 200.0**2)
ENS_SCALE = 1.0 / ((MEM - 1) * STATIC_VAR)


def split(value):
    hi = value.astype(BF16)
    lo = (value - hi.astype(F32)).astype(BF16)
    return hi, lo


def half_first(value):
    first = value[:, 0:OBS] * 0.5
    return first if value.shape[1] == OBS else jnp.concatenate([first, value[:, OBS:]], axis=1)


def rows_of(rows):
    ids = lax.broadcasted_iota(jnp.int32, (16, OBS), 0)
    out = jnp.zeros((16, OBS), F32)
    for place, row in enumerate(rows):
        out = jnp.where(ids == place, jnp.broadcast_to(row, (16, OBS)), out)
    return out.astype(BF16)


def position_parts(crd, place):
    x = crd[0:1, :].astype(F32)
    y = crd[1:2, :].astype(F32)
    base = jnp.full((1, OBS), jnp.asarray(place - NX // 2).astype(F32) * 64.0, F32)
    full = x + base
    square = full * full + y * y
    s1 = square.astype(BF16).astype(F32)
    s2 = (square - s1).astype(BF16).astype(F32)
    s3 = square - s1 - s2
    return s1, s2, s3, base, x, y


def kernel(
    innov, ens, coords, obs, cols, w_out, r_out,
    ens_v, crd_v, v_v, obs_v, cols_v,
    lhsx, rhs, kmat, zx, zf, maskx,
    ens_lo, ens_hi, crd_lo, crd_hi, v_lo, v_hi, p_lo, p_hi,
    part_a, part_b, red_a, red_b,
    load_sem, halo_send, halo_recv, send_a, recv_a, send_b, recv_b,
):
    me = lax.axis_index("region") * 4 + lax.axis_index("sub")

    def device(index):
        return (lax.div(index, 4), lax.rem(index, 4))

    left = device(lax.rem(me + 255, 256))
    right = device(lax.rem(me + 1, 256))
    x = lax.rem(me, 4)
    core = lax.rem(lax.div(me, 4), 2)
    y = lax.rem(lax.div(me, 8), 4)
    z = lax.div(me, 32)

    def peer_a(step):
        there = lax.rem(y * 4 + x + step, 16)
        return device(((z * 4 + lax.div(there, 4)) * 2 + core) * 4 + lax.rem(there, 4))

    def peer_b(step):
        there = lax.rem(z * 2 + core + step, 16)
        return device(((lax.div(there, 2) * 4 + y) * 2 + lax.rem(there, 2)) * 4 + x)

    barrier = pltpu.get_barrier_semaphore()
    for there in (left, right):
        pl.semaphore_signal(barrier, inc=1, device_id=there, device_id_type=MESH)

    def greet(step, carry):
        pl.semaphore_signal(barrier, inc=1, device_id=peer_a(step), device_id_type=MESH)
        pl.semaphore_signal(barrier, inc=1, device_id=peer_b(step), device_id_type=MESH)
        return carry

    lax.fori_loop(1, 16, greet, 0)
    loads = [
        pltpu.make_async_copy(source, target, load_sem.at[i])
        for i, (source, target) in enumerate(
            ((cols, cols_v), (coords, crd_v), (ens, ens_v), (innov, v_v), (obs, obs_v))
        )
    ]
    for load in loads:
        load.start()
    pl.semaphore_wait(barrier, 32)

    def remote(src, dst, slot, there):
        return pltpu.make_async_remote_copy(
            src_ref=src, dst_ref=dst, send_sem=halo_send.at[slot], recv_sem=halo_recv.at[slot],
            device_id=there, device_id_type=MESH,
        )

    small = [
        remote(coords.at[NB - W : NB], crd_lo, 0, right),
        remote(coords.at[0:W], crd_hi, 1, left),
        remote(innov.at[NB - W : NB], v_lo, 2, right),
        remote(innov.at[0:W], v_hi, 3, left),
    ]
    blocks = [
        (
            remote(ens.at[NB - 1 - q], ens_lo.at[W - 1 - q], 4 + 2 * q, right),
            remote(ens.at[q], ens_hi.at[q], 5 + 2 * q, left),
        )
        for q in range(W)
    ]
    for copy in small:
        copy.start()
    for pair in blocks:
        for copy in pair:
            copy.start()
    for load in loads:
        load.wait()

    offset = cols_v[...] - (lax.broadcasted_iota(jnp.int32, (NB, SLOTS), 0) + me * NB)
    for slot in range(SLOTS):
        hit = jnp.max(jnp.where(offset == slot - W, 1.0, 0.0).astype(F32), axis=1, keepdims=True)
        maskx[slot] = jnp.broadcast_to(hit, (NB, OBS))

    def lanes(place, count=1):
        return pl.ds(pl.multiple_of(place * OBS, OBS), count * OBS)

    def set_vectors(place, vectors):
        hi, lo = split(vectors)
        zx[0:16, lanes(place)] = hi
        zx[16:32, lanes(place)] = lo

    def set_left(place, members, crd):
        hi, lo = split(members)
        s1, s2, s3, base, x, y = position_parts(crd, place)
        one = jnp.ones((1, OBS), F32)
        parts = rows_of([s1, s2, s3, one, one, one, base, base, x, x, y])
        stacked = jnp.concatenate([hi, hi, lo, parts, jnp.zeros((48, OBS), BF16)], axis=0)
        lhsx[place - W] = stacked.T

    def set_right(place, members, crd):
        hi, lo = split(members * ENS_SCALE)
        s1, s2, s3, base, x, y = position_parts(crd, place)
        one = jnp.ones((1, OBS), F32)
        parts = rows_of([one, one, one, s1, s2, s3, -2.0 * base, -2.0 * x, -2.0 * base, -2.0 * x, -2.0 * y])
        rhs[place, 0:64, 0:128] = hi
        rhs[place, 64:128, 0:128] = lo
        rhs[place, 128:192, 0:128] = hi
        rhs[place, 192:256, 0:128] = jnp.zeros((64, OBS), BF16)
        rhs[place, 0:192, 128:256] = jnp.zeros((192, OBS), BF16)
        rhs[place, 192:208, 128:256] = parts
        rhs[place, 208:256, 128:256] = jnp.zeros((48, OBS), BF16)

    def prepare_own(i, carry):
        members = ens_v[i]
        vectors = v_v[i]
        set_left(i + W, members, crd_v[i])
        set_right(i + W, members, crd_v[i])
        set_vectors(i + W, vectors)
        zf[0:16, lanes(i)] = vectors
        zf[16:32, lanes(i)] = obs_v[pl.ds(i, 1), :] * vectors
        return carry

    lax.fori_loop(0, NB, prepare_own, 0)

    def tile(b, j, mask):
        both = jnp.dot(lhsx[b + j - W], rhs[b], preferred_element_type=F32)
        shared = both[:, 0:128]
        square = both[:, 128:256]
        inverse = lax.rsqrt(jnp.maximum(square, 1e-30))
        value = jnp.exp2(square * C_CORR * inverse) + jnp.exp2(square * C_LOC) * shared
        hi, lo = split(value * mask)
        kmat[b, j * OBS : (j + 1) * OBS, 0:128] = hi
        kmat[b, j * OBS : (j + 1) * OBS, 128:256] = lo

    def own_mask(b, j):
        return maskx[j + W, pl.ds(b - W, 1), :]

    def add(row, place, count, part):
        part = part[0:16] + part[16:32]
        zf[row : row + 16, lanes(place - W, count)] += part * STATIC_VAR

    def gather(b, start, stop, row):
        vectors = zx[row : row + 32, lanes(b + start, stop - start)]
        if row and start == 0:
            vectors = half_first(vectors)
        part = jnp.dot(
            vectors, kmat[b, start * OBS : stop * OBS, :],
            preferred_element_type=F32,
        )
        add(row // 2 + 16, b, 1, part[:, 0:128] + part[:, 128:256])

    def scatter(b, start, stop, row):
        vectors = zx[row : row + 32, lanes(b)]
        part = lax.dot_general(
            jnp.concatenate([vectors, vectors], axis=1), kmat[b, start * OBS : stop * OBS, :],
            (((1,), (1,)), ((), ())), preferred_element_type=F32,
        )
        if row and start == 0:
            part = half_first(part)
        add(row // 2 + 16, b + start, stop - start, part)

    last = NB

    def edge(b, carry):
        for j in range(HALF):
            tile(b, j, own_mask(b, j))
        gather(b, 0, HALF, 0)
        scatter(b, 1, HALF, 0)
        return carry

    lax.fori_loop(W, 2 * W + EARLY, edge, 0)
    for b in range(last - W, last):
        for j in range(last - b, HALF):
            tile(b, j, own_mask(b, j))
        scatter(b, last - b, HALF, 0)
    for b in range(last, last + W):
        inside = last + W - b
        for j in range(inside):
            tile(b, j, own_mask(b, j))
        gather(b, 0, inside, 0)
        if inside > 1:
            scatter(b, 1, inside, 0)

    for copy in small:
        copy.wait()
    for q in range(W):
        set_vectors(q, v_lo[q])
        set_vectors(q + NB + W, v_hi[q])
    for q in range(W):
        for copy in blocks[q]:
            copy.wait()
        low, high = W - 1 - q, last + W + q
        set_right(low, ens_lo[low], crd_lo[low])
        set_left(high, ens_hi[q], crd_hi[q])
        for j in range(q + 1, HALF):
            c = low + j
            tile(low, j, maskx[W - j, c - W : c - W + 1, :])
            tile(high - j, j, own_mask(high - j, j))
        scatter(low, q + 1, HALF, 0)
        for j in range(q + 1, HALF):
            gather(high - j, j, j + 1, 0)

    moving = [
        remote(zf.at[16:32, 0 : W * OBS], p_hi, 12, left),
        remote(zf.at[16:32, (NB - W) * OBS : NB * OBS], p_lo, 13, right),
    ]
    for copy in moving:
        copy.start()

    lax.fori_loop(2 * W + EARLY, last - W, edge, 0)
    for b in range(last - W, last):
        for j in range(last - b):
            tile(b, j, own_mask(b, j))
        gather(b, 0, HALF, 0)
        if last - b > 1:
            scatter(b, 1, last - b, 0)

    def renew(row, source, start):
        hi, lo = split(source)
        zx[row : row + 16, start * OBS : start * OBS + source.shape[1]] = hi
        zx[row + 16 : row + 32, start * OBS : start * OBS + source.shape[1]] = lo

    renew(32, zf[16:32, :], W)

    def upper(b, carry):
        zf[32:48, lanes(b - W)] = 0.5 * obs_v[pl.ds(b - W, 1), :] * zf[16:32, lanes(b - W)]
        gather(b, 0, HALF, 32)
        return carry

    lax.fori_loop(W, last, upper, 0)
    for b in range(last, last + W):
        upper_lanes = lanes(b - W)
        zf[32:48, upper_lanes] = 0.5 * obs_v[b - W : b - W + 1, :] * zf[16:32, upper_lanes]
        gather(b, 0, last + W - b, 32)
    for copy in moving:
        copy.wait()
    renew(32, p_hi[...], NB + W)
    for b in range(last, last + W):
        gather(b, last + W - b, HALF, 32)
    renew(64, zf[32:48, :], W)

    inner = slice(W * OBS, (W + NB) * OBS)
    gram = lax.dot_general(
        zx[0:64, inner], zx[0:96, inner], (((1,), (1,)), ((), ())), preferred_element_type=F32
    )
    gram = jnp.concatenate([gram, jnp.zeros((64, 32), F32)], axis=1)
    lane = lax.broadcasted_iota(jnp.int32, (16, OBS), 1)
    lane8 = lax.broadcasted_iota(jnp.int32, (8, OBS), 1)

    def turn(value, by):
        return pltpu.roll(value, by % OBS, 1)

    of_r = gram[0:16] + gram[16:32]
    of_p = gram[32:48] + gram[48:64]
    of_r = of_r + turn(of_r, -16)
    of_p = of_p + turn(of_p, -16)
    even = (lane & 16) == 0
    own_part = jnp.where(even, of_r, turn(of_p, -16))
    part_a[...] = jnp.where(lane8 < 64, own_part[0:8], turn(own_part[8:16], 64))

    def exchange(part, red, peer, send, recv):
        copies = [
            pltpu.make_async_remote_copy(
                src_ref=part, dst_ref=red.at[step - 1], send_sem=send.at[step - 1], recv_sem=recv.at[step - 1],
                device_id=peer(step), device_id_type=MESH,
            )
            for step in range(1, 16)
        ]
        for copy in copies:
            copy.start()
        return copies

    first_sum = exchange(part_a, red_a, peer_a, send_a, recv_a)

    def rest(b, carry):
        scatter(b, 0, HALF, 32)
        return carry

    renew(32, p_lo[...], 0)
    for b in range(W):
        scatter(b, W - b, HALF, 32)
    lax.fori_loop(W, last, rest, 0)
    for b in range(last, last + W):
        scatter(b, 0, last + W - b, 32)

    def other_half(i, carry):
        zf[32:48, lanes(i)] += 0.5 * obs_v[pl.ds(i, 1), :] * zf[16:32, lanes(i)]
        return carry

    lax.fori_loop(0, NB, other_half, 0)
    for copy in first_sum:
        copy.wait()
    part_b[...] = part_a[...] + jnp.sum(red_a[...], axis=0)
    second_sum = exchange(part_b, red_b, peer_b, send_b, recv_b)
    for copy in second_sum:
        copy.wait()
    packed = part_b[...] + jnp.sum(red_b[...], axis=0)

    moments = jnp.concatenate([packed, turn(packed, 64)], axis=0)
    top = jnp.where(lane < 16, turn(moments, -32), jnp.where(lane < 32, moments, turn(moments, 32)))
    low = jnp.where(lane < 16, turn(moments, -16), jnp.where(lane < 32, turn(moments, -32), moments))
    system = jnp.concatenate([top, low], axis=0)
    rows = lax.broadcasted_iota(jnp.int32, (32, OBS), 0)
    half = jnp.where((lane >= 16) & (lane < 32), system[16:32], 0.0)
    flipped = jnp.concatenate([half, jnp.zeros((112, OBS), F32)], axis=0).T[16:32, :]
    system = jnp.concatenate([system[0:16], system[16:32] + turn(flipped, 16)], axis=0)
    spread = [jnp.broadcast_to(system[:, j : j + 1], (32, OBS)) for j in range(32)]
    inverses = []
    for k in range(32):
        inverse = 1.0 / spread[k][k : k + 1, :]
        factor = jnp.where(rows == k, 0.0, spread[k] * inverse)
        for j in range(k + 1, 32):
            spread[j] = spread[j] - factor * spread[j][k : k + 1, :]
        system = system - factor * system[k : k + 1, :]
        inverses.append(inverse)
    system = system * jnp.concatenate(inverses, axis=0)

    solved = jnp.concatenate([system, jnp.zeros((96, OBS), F32)], axis=0).T
    for_w = jnp.where(lane < 32, solved[32:48, :], 0.0)
    both = jnp.concatenate([for_w, turn(for_w, 16)], axis=0)[:, 0:48]
    for chunk in range(4):
        here = slice(chunk * 4 * OBS, (chunk + 1) * 4 * OBS)
        sums = jnp.dot(both, zf[:, here], preferred_element_type=F32, precision=lax.Precision.HIGHEST)
        left_over = zf[0:16, here] - sums[16:32]
        for piece in range(4):
            b = chunk * 4 + piece
            w_out[b] = sums[0:16, piece * OBS : (piece + 1) * OBS]
            r_out[b] = left_over[:, piece * OBS : (piece + 1) * OBS]


def on_device(innovations, ensemble, coords, obs_error, pair_cols, pair_count):
    del pair_count
    vmem = pl.BlockSpec(memory_space=pltpu.VMEM)
    arrays = [pltpu.with_memory_space_constraint(a, pltpu.HBM) for a in (innovations, ensemble, coords, obs_error, pair_cols)]
    out = jax.ShapeDtypeStruct((NB, RHS, OBS), F32)
    return pl.pallas_call(
        kernel,
        out_shape=(out, out),
        in_specs=[pl.BlockSpec(memory_space=pltpu.HBM)] * 5,
        out_specs=(vmem, vmem),
        scratch_shapes=[
            pltpu.VMEM((NB, MEM, OBS), F32),
            pltpu.VMEM((NB, 2, OBS), jnp.int32),
            pltpu.VMEM((NB, RHS, OBS), F32),
            pltpu.VMEM((NB, OBS), F32),
            pltpu.VMEM((NB, SLOTS), jnp.int32),
            pltpu.VMEM((NB + W, OBS, 256), BF16),
            pltpu.VMEM((NB + W, 256, 256), BF16),
            pltpu.VMEM((NB + W, HALF * OBS, 256), BF16),
            pltpu.VMEM((96, NX * OBS), BF16),
            pltpu.VMEM((48, NB * OBS), F32),
            pltpu.VMEM((SLOTS, NB, OBS), F32),
            pltpu.VMEM((W, MEM, OBS), F32),
            pltpu.VMEM((W, MEM, OBS), F32),
            pltpu.VMEM((W, 2, OBS), jnp.int32),
            pltpu.VMEM((W, 2, OBS), jnp.int32),
            pltpu.VMEM((W, RHS, OBS), F32),
            pltpu.VMEM((W, RHS, OBS), F32),
            pltpu.VMEM((RHS, W * OBS), F32),
            pltpu.VMEM((RHS, W * OBS), F32),
            pltpu.VMEM((8, OBS), F32),
            pltpu.VMEM((8, OBS), F32),
            pltpu.VMEM((15, 8, OBS), F32),
            pltpu.VMEM((15, 8, OBS), F32),
            pltpu.SemaphoreType.DMA((5,)),
            pltpu.SemaphoreType.DMA((14,)),
            pltpu.SemaphoreType.DMA((14,)),
            pltpu.SemaphoreType.DMA((15,)),
            pltpu.SemaphoreType.DMA((15,)),
            pltpu.SemaphoreType.DMA((15,)),
            pltpu.SemaphoreType.DMA((15,)),
        ],
        compiler_params=pltpu.CompilerParams(
            collective_id=0, has_side_effects=True, vmem_limit_bytes=LIMIT
        ),
    )(*arrays)


def solution(mesh):
    both = ("region", "sub")
    in_specs = (
        P(both, None, None),
        P(both, None, None),
        P(both, None, None),
        P(both, None),
        P(both, None),
        P(both),
    )
    out_specs = (P(both, None, None), P(both, None, None))
    return jax.shard_map(on_device, mesh=mesh, in_specs=in_specs, out_specs=out_specs, check_vma=False)
```

profile of v0, /device:TPU:1, one launch (start us, length us, event | category | flops | bytes accessed | tf_op | source)
XLA Modules:
  0.0 39.4 jit_solution(7004114785593798649)
XLA Ops:
  0.6 37.5 %shard_map.68 = (f32[16,16,128]{2,1,0:T(8,128)S(1)}, f32[16,16,128]{2,1,0:T(8,128)S(1)}) custom-call(f32[16,16,128]{2,1,0:T(8,128)} %innov.1, f32[16,64,128]{2,1,0:T(8,128)} %ens.1, s32[16,2,128]{2,1,0:T(2,128)} %coords.1, f32[16,128]{1,0:T(8,128)} %obs.1, s32[16,9]{1,0:T(8,128)} %cols.1), custom_call_target="tpu_custom_call" | custom-call | tf_op jit(solution)/shard_map/pallas_call | solution.py:393
  38.1 0.7 %copy.9 = f32[16,16,128]{2,1,0:T(8,128)} copy(f32[16,16,128]{2,1,0:T(8,128)S(1)} %get-tuple-element.4) | data formatting | bytes 262144
  38.8 0.7 %copy.10 = f32[16,16,128]{2,1,0:T(8,128)} copy(f32[16,16,128]{2,1,0:T(8,128)S(1)} %get-tuple-element.5) | data formatting | bytes 262144
where the time goes:
time: 39.5 us; the launch traced here: 39.4 us
  Pallas kernels  37.5 us (95%)
  local copies, waits for them, and re-layouts  1.31 us (3%)
  between operations  0.64 us (2%)
    pallas_call x1, Pallas kernels, on_device(): pl.pallas_call(kernel, out_shape=(out, out), in_specs=[pl.BlockSpec(memor...  37.5 us
    unnamed x2, local copies, waits for them, and re-layouts  1.31 us

commit v1 on v0

--- a/solution.py
+++ b/solution.py
@@ -10,7 +10,8 @@
 BF16 = jnp.bfloat16
 
 LIMIT = 40 * 1024 * 1024
-EARLY = 2
+UNROLL = 4
+EARLY = 3
 NB = 16
 W = 4
 NX = NB + 2 * W
@@ -152,7 +153,7 @@
         one = jnp.ones((1, OBS), F32)
         parts = rows_of([s1, s2, s3, one, one, one, base, base, x, x, y])
         stacked = jnp.concatenate([hi, hi, lo, parts, jnp.zeros((48, OBS), BF16)], axis=0)
-        lhsx[place - W] = stacked.T
+        lhsx[pl.ds(pl.multiple_of((place - W) * OBS, OBS), OBS), :] = stacked.T
 
     def set_right(place, members, crd):
         hi, lo = split(members * ENS_SCALE)
@@ -179,18 +180,25 @@
 
     lax.fori_loop(0, NB, prepare_own, 0)
 
-    def tile(b, j, mask):
-        both = jnp.dot(lhsx[b + j - W], rhs[b], preferred_element_type=F32)
-        shared = both[:, 0:128]
-        square = both[:, 128:256]
-        inverse = lax.rsqrt(jnp.maximum(square, 1e-30))
-        value = jnp.exp2(square * C_CORR * inverse) + jnp.exp2(square * C_LOC) * shared
-        hi, lo = split(value * mask)
-        kmat[b, j * OBS : (j + 1) * OBS, 0:128] = hi
-        kmat[b, j * OBS : (j + 1) * OBS, 128:256] = lo
+    def tiles(b, start, stop, mask):
+        count = stop - start
+        here = pl.ds(pl.multiple_of((b + start - W) * OBS, OBS), count * OBS)
+        every = jnp.dot(lhsx[here, :], rhs[b], preferred_element_type=F32)
+        for j in range(start, stop):
+            both = every[(j - start) * OBS : (j - start + 1) * OBS]
+            shared = both[:, 0:128]
+            square = both[:, 128:256]
+            inverse = lax.rsqrt(jnp.maximum(square, 1e-30))
+            value = jnp.exp2(square * C_CORR * inverse) + jnp.exp2(square * C_LOC) * shared
+            hi, lo = split(value * mask(b, j))
+            kmat[b, j * OBS : (j + 1) * OBS, 0:128] = hi
+            kmat[b, j * OBS : (j + 1) * OBS, 128:256] = lo
 
     def own_mask(b, j):
         return maskx[j + W, pl.ds(b - W, 1), :]
+
+    def low_mask(b, j):
+        return maskx[W - j, b + j - W : b + j - W + 1, :]
 
     def add(row, place, count, part):
         part = part[0:16] + part[16:32]
@@ -218,25 +226,29 @@
 
     last = NB
 
-    def edge(b, carry):
-        for j in range(HALF):
-            tile(b, j, own_mask(b, j))
-        gather(b, 0, HALF, 0)
-        scatter(b, 1, HALF, 0)
-        return carry
-
-    lax.fori_loop(W, 2 * W + EARLY, edge, 0)
-    for b in range(last - W, last):
-        for j in range(last - b, HALF):
-            tile(b, j, own_mask(b, j))
-        scatter(b, last - b, HALF, 0)
-    for b in range(last, last + W):
-        inside = last + W - b
-        for j in range(inside):
-            tile(b, j, own_mask(b, j))
+    def apply_to(b, inside):
         gather(b, 0, inside, 0)
         if inside > 1:
             scatter(b, 1, inside, 0)
+
+    def step(b, carry):
+        apply_to(b - 1, HALF)
+        tiles(b, 0, HALF, own_mask)
+        return carry
+
+    tiles(W, 0, HALF, own_mask)
+    lax.fori_loop(W + 1, 2 * W + EARLY, step, 0)
+    tiles(last - W, W, HALF, own_mask)
+    apply_to(2 * W + EARLY - 1, HALF)
+    for b in range(last - W + 1, last):
+        tiles(b, last - b, HALF, own_mask)
+        scatter(b - 1, last + 1 - b, HALF, 0)
+    tiles(last, 0, W, own_mask)
+    scatter(last - 1, 1, HALF, 0)
+    for b in range(last + 1, last + W):
+        tiles(b, 0, last + W - b, own_mask)
+        apply_to(b - 1, last + W + 1 - b)
+    apply_to(last + W - 1, 1)
 
     for copy in small:
         copy.wait()
@@ -249,10 +261,9 @@
         low, high = W - 1 - q, last + W + q
         set_right(low, ens_lo[low], crd_lo[low])
         set_left(high, ens_hi[q], crd_hi[q])
+        tiles(low, q + 1, HALF, low_mask)
         for j in range(q + 1, HALF):
-            c = low + j
-            tile(low, j, maskx[W - j, c - W : c - W + 1, :])
-            tile(high - j, j, own_mask(high - j, j))
+            tiles(high - j, j, j + 1, own_mask)
         scatter(low, q + 1, HALF, 0)
         for j in range(q + 1, HALF):
             gather(high - j, j, j + 1, 0)
@@ -264,13 +275,15 @@
     for copy in moving:
         copy.start()
 
-    lax.fori_loop(2 * W + EARLY, last - W, edge, 0)
-    for b in range(last - W, last):
-        for j in range(last - b):
-            tile(b, j, own_mask(b, j))
-        gather(b, 0, HALF, 0)
-        if last - b > 1:
-            scatter(b, 1, last - b, 0)
+    tiles(2 * W + EARLY, 0, HALF, own_mask)
+    lax.fori_loop(2 * W + EARLY + 1, last - W, step, 0)
+    tiles(last - W, 0, W, own_mask)
+    apply_to(last - W - 1, HALF)
+    for b in range(last - W + 1, last):
+        tiles(b, 0, last - b, own_mask)
+        gather(b - 1, 0, HALF, 0)
+        scatter(b - 1, 1, last + 1 - b, 0)
+    gather(last - 1, 0, HALF, 0)
 
     def renew(row, source, start):
         hi, lo = split(source)
@@ -279,40 +292,53 @@
 
     renew(32, zf[16:32, :], W)
 
-    def upper(b, carry):
+    def upper(b):
         zf[32:48, lanes(b - W)] = 0.5 * obs_v[pl.ds(b - W, 1), :] * zf[16:32, lanes(b - W)]
         gather(b, 0, HALF, 32)
-        return carry
-
-    lax.fori_loop(W, last, upper, 0)
+
+    def uppers(i, carry):
+        for more in range(UNROLL):
+            upper(W + i * UNROLL + more)
+        return carry
+
+    lax.fori_loop(0, (last - W) // UNROLL, uppers, 0)
     for b in range(last, last + W):
         upper_lanes = lanes(b - W)
         zf[32:48, upper_lanes] = 0.5 * obs_v[b - W : b - W + 1, :] * zf[16:32, upper_lanes]
         gather(b, 0, last + W - b, 32)
+    lane = lax.broadcasted_iota(jnp.int32, (16, OBS), 1)
+    lane8 = lax.broadcasted_iota(jnp.int32, (8, OBS), 1)
+
+    def turn(value, by):
+        return pltpu.roll(value, by % OBS, 1)
+
+    def columns_gram(row, row_end, col, col_end, inner):
+        value = lax.dot_general(
+            zx[row:row_end, inner], zx[col:col_end, inner], (((1,), (1,)), ((), ())), preferred_element_type=F32
+        )
+        if col:
+            value = jnp.concatenate([jnp.zeros((row_end - row, col), F32), value], axis=1)
+        return jnp.concatenate([value, jnp.zeros((row_end - row, OBS - col_end), F32)], axis=1)
+
+    def fold(value):
+        value = value[0:16] + value[16:32]
+        return value + turn(value, -16)
+
+    renew(64, zf[32:48, 0 : (NB - W) * OBS], W)
+    known = columns_gram(0, 64, 0, 64, slice(W * OBS, (W + NB) * OBS))
+    of_r = fold(known[0:32])
+    first_gram = known[32:64] + columns_gram(32, 64, 64, 96, slice(W * OBS, last * OBS))
+    even = (lane & 16) == 0
     for copy in moving:
         copy.wait()
     renew(32, p_hi[...], NB + W)
     for b in range(last, last + W):
         gather(b, last + W - b, HALF, 32)
-    renew(64, zf[32:48, :], W)
-
-    inner = slice(W * OBS, (W + NB) * OBS)
-    gram = lax.dot_general(
-        zx[0:64, inner], zx[0:96, inner], (((1,), (1,)), ((), ())), preferred_element_type=F32
-    )
-    gram = jnp.concatenate([gram, jnp.zeros((64, 32), F32)], axis=1)
-    lane = lax.broadcasted_iota(jnp.int32, (16, OBS), 1)
-    lane8 = lax.broadcasted_iota(jnp.int32, (8, OBS), 1)
-
-    def turn(value, by):
-        return pltpu.roll(value, by % OBS, 1)
-
-    of_r = gram[0:16] + gram[16:32]
-    of_p = gram[32:48] + gram[48:64]
-    of_r = of_r + turn(of_r, -16)
-    of_p = of_p + turn(of_p, -16)
-    even = (lane & 16) == 0
-    own_part = jnp.where(even, of_r, turn(of_p, -16))
+    renew(64, zf[32:48, (NB - W) * OBS :], last)
+
+    late = slice(last * OBS, (last + W) * OBS)
+    total = first_gram + columns_gram(32, 64, 64, 96, late)
+    own_part = jnp.where(even, of_r, turn(fold(total), -16))
     part_a[...] = jnp.where(lane8 < 64, own_part[0:8], turn(own_part[8:16], 64))
 
     def exchange(part, red, peer, send, recv):
@@ -329,14 +355,15 @@
 
     first_sum = exchange(part_a, red_a, peer_a, send_a, recv_a)
 
-    def rest(b, carry):
-        scatter(b, 0, HALF, 32)
+    def rest(i, carry):
+        for more in range(UNROLL):
+            scatter(W + i * UNROLL + more, 0, HALF, 32)
         return carry
 
     renew(32, p_lo[...], 0)
     for b in range(W):
         scatter(b, W - b, HALF, 32)
-    lax.fori_loop(W, last, rest, 0)
+    lax.fori_loop(0, (last - W) // UNROLL, rest, 0)
     for b in range(last, last + W):
         scatter(b, 0, last + W - b, 32)
 
@@ -401,7 +428,7 @@
             pltpu.VMEM((NB, RHS, OBS), F32),
             pltpu.VMEM((NB, OBS), F32),
             pltpu.VMEM((NB, SLOTS), jnp.int32),
-            pltpu.VMEM((NB + W, OBS, 256), BF16),
+            pltpu.VMEM(((NB + W) * OBS, 256), BF16),
             pltpu.VMEM((NB + W, 256, 256), BF16),
             pltpu.VMEM((NB + W, HALF * OBS, 256), BF16),
             pltpu.VMEM((96, NX * OBS), BF16),

time: 39.5 us -> 37 us (0.937)
  Pallas kernels: 37.5 us -> 34.9 us
    pallas_call x1, Pallas kernels: 37.5 us -> 34.9 us  [on_device(): pl.pallas_call(kernel, out_shape=(out, out), in_specs=[pl.BlockSpec(memor...]
where the time goes in v1:
time: 37 us; the launch traced here: 36.9 us
  Pallas kernels  34.9 us (94%)
  local copies, waits for them, and re-layouts  1.31 us (4%)
  between operations  0.64 us (2%)
    pallas_call x1, Pallas kernels, on_device(): pl.pallas_call(kernel, out_shape=(out, out), in_specs=[pl.BlockSpec(memor...  34.9 us
    unnamed x2, local copies, waits for them, and re-layouts  1.31 us

profile of v1, /device:TPU:1, one launch (start us, length us, event | category | flops | bytes accessed | tf_op | source)
XLA Modules:
  0.0 36.9 jit_solution(6101355669222589443)
XLA Ops:
  0.6 34.9 %shard_map.68 = (f32[16,16,128]{2,1,0:T(8,128)S(1)}, f32[16,16,128]{2,1,0:T(8,128)S(1)}) custom-call(f32[16,16,128]{2,1,0:T(8,128)} %innov.1, f32[16,64,128]{2,1,0:T(8,128)} %ens.1, s32[16,2,128]{2,1,0:T(2,128)} %coords.1, f32[16,128]{1,0:T(8,128)} %obs.1, s32[16,9]{1,0:T(8,128)} %cols.1), custom_call_target="tpu_custom_call" | custom-call | tf_op jit(solution)/shard_map/pallas_call | solution.py:420
  35.6 0.7 %copy.9 = f32[16,16,128]{2,1,0:T(8,128)} copy(f32[16,16,128]{2,1,0:T(8,128)S(1)} %get-tuple-element.4) | data formatting | bytes 262144
  36.2 0.7 %copy.10 = f32[16,16,128]{2,1,0:T(8,128)} copy(f32[16,16,128]{2,1,0:T(8,128)S(1)} %get-tuple-element.5) | data formatting | bytes 262144

commit v2 on v1

--- a/solution.py
+++ b/solution.py
@@ -87,16 +87,6 @@
         there = lax.rem(z * 2 + core + step, 16)
         return device(((lax.div(there, 2) * 4 + y) * 2 + lax.rem(there, 2)) * 4 + x)
 
-    barrier = pltpu.get_barrier_semaphore()
-    for there in (left, right):
-        pl.semaphore_signal(barrier, inc=1, device_id=there, device_id_type=MESH)
-
-    def greet(step, carry):
-        pl.semaphore_signal(barrier, inc=1, device_id=peer_a(step), device_id_type=MESH)
-        pl.semaphore_signal(barrier, inc=1, device_id=peer_b(step), device_id_type=MESH)
-        return carry
-
-    lax.fori_loop(1, 16, greet, 0)
     loads = [
         pltpu.make_async_copy(source, target, load_sem.at[i])
         for i, (source, target) in enumerate(
@@ -105,6 +95,13 @@
     ]
     for load in loads:
         load.start()
+    barrier = pltpu.get_barrier_semaphore()
+    for there in (left, right):
+        pl.semaphore_signal(barrier, inc=1, device_id=there, device_id_type=MESH)
+
+    for step in range(1, 16):
+        pl.semaphore_signal(barrier, inc=1, device_id=peer_a(step), device_id_type=MESH)
+        pl.semaphore_signal(barrier, inc=1, device_id=peer_b(step), device_id_type=MESH)
     pl.semaphore_wait(barrier, 32)
 
     def remote(src, dst, slot, there):
@@ -250,30 +247,35 @@
         apply_to(b - 1, last + W + 1 - b)
     apply_to(last + W - 1, 1)
 
-    for copy in small:
-        copy.wait()
+    small[0].wait()
+    small[2].wait()
     for q in range(W):
         set_vectors(q, v_lo[q])
+    for q in range(W):
+        low = W - 1 - q
+        blocks[q][0].wait()
+        set_right(low, ens_lo[low], crd_lo[low])
+        tiles(low, q + 1, HALF, low_mask)
+        if q:
+            scatter(low + 1, q, HALF, 0)
+    scatter(0, W, HALF, 0)
+    to_left = remote(zf.at[16:32, 0 : W * OBS], p_hi, 12, left)
+    to_left.start()
+
+    small[1].wait()
+    small[3].wait()
+    for q in range(W):
         set_vectors(q + NB + W, v_hi[q])
     for q in range(W):
-        for copy in blocks[q]:
-            copy.wait()
-        low, high = W - 1 - q, last + W + q
-        set_right(low, ens_lo[low], crd_lo[low])
+        high = last + W + q
+        blocks[q][1].wait()
         set_left(high, ens_hi[q], crd_hi[q])
-        tiles(low, q + 1, HALF, low_mask)
         for j in range(q + 1, HALF):
             tiles(high - j, j, j + 1, own_mask)
-        scatter(low, q + 1, HALF, 0)
-        for j in range(q + 1, HALF):
-            gather(high - j, j, j + 1, 0)
-
-    moving = [
-        remote(zf.at[16:32, 0 : W * OBS], p_hi, 12, left),
-        remote(zf.at[16:32, (NB - W) * OBS : NB * OBS], p_lo, 13, right),
-    ]
-    for copy in moving:
-        copy.start()
+    for b in range(last, last + W):
+        gather(b, last + W - b, HALF, 0)
+    to_right = remote(zf.at[16:32, (NB - W) * OBS : NB * OBS], p_lo, 13, right)
+    to_right.start()
 
     tiles(2 * W + EARLY, 0, HALF, own_mask)
     lax.fori_loop(2 * W + EARLY + 1, last - W, step, 0)
@@ -312,33 +314,39 @@
     def turn(value, by):
         return pltpu.roll(value, by % OBS, 1)
 
-    def columns_gram(row, row_end, col, col_end, inner):
-        value = lax.dot_general(
-            zx[row:row_end, inner], zx[col:col_end, inner], (((1,), (1,)), ((), ())), preferred_element_type=F32
-        )
-        if col:
-            value = jnp.concatenate([jnp.zeros((row_end - row, col), F32), value], axis=1)
-        return jnp.concatenate([value, jnp.zeros((row_end - row, OBS - col_end), F32)], axis=1)
-
-    def fold(value):
-        value = value[0:16] + value[16:32]
-        return value + turn(value, -16)
-
-    renew(64, zf[32:48, 0 : (NB - W) * OBS], W)
-    known = columns_gram(0, 64, 0, 64, slice(W * OBS, (W + NB) * OBS))
-    of_r = fold(known[0:32])
-    first_gram = known[32:64] + columns_gram(32, 64, 64, 96, slice(W * OBS, last * OBS))
-    even = (lane & 16) == 0
-    for copy in moving:
-        copy.wait()
-    renew(32, p_hi[...], NB + W)
+    def product_gram(left_rows, right_rows):
+        value = lax.dot_general(left_rows, right_rows, (((1,), (1,)), ((), ())), preferred_element_type=F32)
+        height, width = value.shape
+        value = jnp.concatenate([value, jnp.zeros((height, OBS - width), F32)], axis=1)
+        value = value[0:16] + value[16:32] if height == 32 else value
+        return value + turn(value, -16) if height == 32 else value
+
+    own = slice(W * OBS, (W + NB) * OBS)
+    renew(64, zf[32:48, :], W)
+    of_r = product_gram(zx[0:32, own], zx[0:64, own])
+    of_p = product_gram(zx[32:64, own], zx[32:96, own])
+    of_h = product_gram(zx[64:96, own], zx[32:64, own])
+    place = lane >> 4
+    early = jnp.where(
+        place == 0, of_r, jnp.where(place == 1, turn(of_p, 16), jnp.where(place == 2, of_r, turn(of_p, 16) + turn(of_h, 48)))
+    )
+    across = [None] * W
     for b in range(last, last + W):
-        gather(b, last + W - b, HALF, 32)
-    renew(64, zf[32:48, (NB - W) * OBS :], last)
-
-    late = slice(last * OBS, (last + W) * OBS)
-    total = first_gram + columns_gram(32, 64, 64, 96, late)
-    own_part = jnp.where(even, of_r, turn(fold(total), -16))
+        start = last + W - b
+        vectors = zx[32:64, b * OBS : (b + 1) * OBS]
+        part = lax.dot_general(
+            jnp.concatenate([vectors, vectors], axis=1), kmat[b, start * OBS :, :],
+            (((1,), (1,)), ((), ())), preferred_element_type=F32,
+        )
+        part = (part[0:16] + part[16:32]) * STATIC_VAR
+        for i in range(HALF - start):
+            piece = part[:, i * OBS : (i + 1) * OBS]
+            across[i] = piece if across[i] is None else across[i] + piece
+    across = jnp.concatenate(split(jnp.concatenate(across, axis=1)), axis=0)
+    to_left.wait()
+    theirs = jnp.concatenate(split(p_hi[...]), axis=0)
+    late = product_gram(across, theirs) + product_gram(theirs, across)
+    own_part = jnp.where(place == 3, early + turn(late, 48), early)
     part_a[...] = jnp.where(lane8 < 64, own_part[0:8], turn(own_part[8:16], 64))
 
     def exchange(part, red, peer, send, recv):
@@ -360,6 +368,10 @@
             scatter(W + i * UNROLL + more, 0, HALF, 32)
         return carry
 
+    renew(32, p_hi[...], NB + W)
+    for b in range(last, last + W):
+        gather(b, last + W - b, HALF, 32)
+    to_right.wait()
     renew(32, p_lo[...], 0)
     for b in range(W):
         scatter(b, W - b, HALF, 32)
@@ -381,14 +393,15 @@
     packed = part_b[...] + jnp.sum(red_b[...], axis=0)
 
     moments = jnp.concatenate([packed, turn(packed, 64)], axis=0)
-    top = jnp.where(lane < 16, turn(moments, -32), jnp.where(lane < 32, moments, turn(moments, 32)))
-    low = jnp.where(lane < 16, turn(moments, -16), jnp.where(lane < 32, turn(moments, -32), moments))
-    system = jnp.concatenate([top, low], axis=0)
     rows = lax.broadcasted_iota(jnp.int32, (32, OBS), 0)
-    half = jnp.where((lane >= 16) & (lane < 32), system[16:32], 0.0)
-    flipped = jnp.concatenate([half, jnp.zeros((112, OBS), F32)], axis=0).T[16:32, :]
-    system = jnp.concatenate([system[0:16], system[16:32] + turn(flipped, 16)], axis=0)
-    spread = [jnp.broadcast_to(system[:, j : j + 1], (32, OBS)) for j in range(32)]
+
+    def column(at):
+        return jnp.broadcast_to(moments[:, at : at + 1], (16, OBS))
+
+    system = jnp.concatenate([moments, turn(moments, -32)], axis=0)
+    middle = [column(16 + j) for j in range(16)]
+    spread = [jnp.concatenate([column(32 + j), middle[j]], axis=0) for j in range(16)]
+    spread += [jnp.concatenate([middle[j], column(48 + j)], axis=0) for j in range(16)]
     inverses = []
     for k in range(32):
         inverse = 1.0 / spread[k][k : k + 1, :]
@@ -400,7 +413,7 @@
     system = system * jnp.concatenate(inverses, axis=0)
 
     solved = jnp.concatenate([system, jnp.zeros((96, OBS), F32)], axis=0).T
-    for_w = jnp.where(lane < 32, solved[32:48, :], 0.0)
+    for_w = jnp.where(lane < 32, solved[0:16, :], 0.0)
     both = jnp.concatenate([for_w, turn(for_w, 16)], axis=0)[:, 0:48]
     for chunk in range(4):
         here = slice(chunk * 4 * OBS, (chunk + 1) * 4 * OBS)

time: 37 us -> 36.2 us (0.978)
  Pallas kernels: 34.9 us -> 34.2 us
    pallas_call x1, Pallas kernels: 34.9 us -> 34.2 us  [on_device(): pl.pallas_call(kernel, out_shape=(out, out), in_specs=[pl.BlockSpec(memor...]
where the time goes in v2:
time: 36.2 us
  Pallas kernels  34.2 us (94%)
  local copies, waits for them, and re-layouts  1.31 us (4%)
  between operations  0.64 us (2%)
    pallas_call x1, Pallas kernels, on_device(): pl.pallas_call(kernel, out_shape=(out, out), in_specs=[pl.BlockSpec(memor...  34.2 us
    unnamed x2, local copies, waits for them, and re-layouts  1.31 us

profile of v2, /device:TPU:1, one launch (start us, length us, event | category | flops | bytes accessed | tf_op | source)
XLA Modules:
  0.0 36.2 jit_solution(8502908565051976993)
XLA Ops:
  0.6 34.2 %shard_map.68 = (f32[16,16,128]{2,1,0:T(8,128)S(1)}, f32[16,16,128]{2,1,0:T(8,128)S(1)}) custom-call(f32[16,16,128]{2,1,0:T(8,128)} %innov.1, f32[16,64,128]{2,1,0:T(8,128)} %ens.1, s32[16,2,128]{2,1,0:T(2,128)} %coords.1, f32[16,128]{1,0:T(8,128)} %obs.1, s32[16,9]{1,0:T(8,128)} %cols.1), custom_call_target="tpu_custom_call" | custom-call | tf_op jit(solution)/shard_map/pallas_call | solution.py:433
  34.8 0.7 %copy.9 = f32[16,16,128]{2,1,0:T(8,128)} copy(f32[16,16,128]{2,1,0:T(8,128)S(1)} %get-tuple-element.4) | data formatting | bytes 262144
  35.5 0.7 %copy.10 = f32[16,16,128]{2,1,0:T(8,128)} copy(f32[16,16,128]{2,1,0:T(8,128)S(1)} %get-tuple-element.5) | data formatting | bytes 262144

commit v3 on v2

--- a/solution.py
+++ b/solution.py
@@ -79,13 +79,20 @@
     y = lax.rem(lax.div(me, 8), 4)
     z = lax.div(me, 32)
 
-    def peer_a(step):
-        there = lax.rem(y * 4 + x + step, 16)
-        return device(((z * 4 + lax.div(there, 4)) * 2 + core) * 4 + lax.rem(there, 4))
-
-    def peer_b(step):
-        there = lax.rem(z * 2 + core + step, 16)
-        return device(((lax.div(there, 2) * 4 + y) * 2 + lax.rem(there, 2)) * 4 + x)
+    def peer_a(dy, dx):
+        return device(((z * 4 + lax.rem(y + dy, 4)) * 2 + core) * 4 + lax.rem(x + dx, 4))
+
+    def peer_b(dz, dc):
+        return device(((lax.rem(z + dz, 8) * 4 + y) * 2 + lax.rem(core + dc, 2)) * 4 + x)
+
+    peers_a = [peer_a(dy, dx) for dy, dx in sorted(
+        ((dy, dx) for dy in range(4) for dx in range(4) if dy or dx),
+        key=lambda by: -min(by[0], 4 - by[0]) - min(by[1], 4 - by[1]),
+    )]
+    peers_b = [peer_b(dz, dc) for dz, dc in sorted(
+        ((dz, dc) for dz in range(8) for dc in range(2) if dz or dc),
+        key=lambda by: -2 * min(by[0], 8 - by[0]) - by[1],
+    )]
 
     loads = [
         pltpu.make_async_copy(source, target, load_sem.at[i])
@@ -99,9 +106,8 @@
     for there in (left, right):
         pl.semaphore_signal(barrier, inc=1, device_id=there, device_id_type=MESH)
 
-    for step in range(1, 16):
-        pl.semaphore_signal(barrier, inc=1, device_id=peer_a(step), device_id_type=MESH)
-        pl.semaphore_signal(barrier, inc=1, device_id=peer_b(step), device_id_type=MESH)
+    for there in peers_b + peers_a:
+        pl.semaphore_signal(barrier, inc=1, device_id=there, device_id_type=MESH)
     pl.semaphore_wait(barrier, 32)
 
     def remote(src, dst, slot, there):
@@ -349,19 +355,19 @@
     own_part = jnp.where(place == 3, early + turn(late, 48), early)
     part_a[...] = jnp.where(lane8 < 64, own_part[0:8], turn(own_part[8:16], 64))
 
-    def exchange(part, red, peer, send, recv):
+    def exchange(part, red, peers, send, recv):
         copies = [
             pltpu.make_async_remote_copy(
-                src_ref=part, dst_ref=red.at[step - 1], send_sem=send.at[step - 1], recv_sem=recv.at[step - 1],
-                device_id=peer(step), device_id_type=MESH,
+                src_ref=part, dst_ref=red.at[i], send_sem=send.at[i], recv_sem=recv.at[i],
+                device_id=there, device_id_type=MESH,
             )
-            for step in range(1, 16)
+            for i, there in enumerate(peers)
         ]
         for copy in copies:
             copy.start()
         return copies
 
-    first_sum = exchange(part_a, red_a, peer_a, send_a, recv_a)
+    first_sum = exchange(part_a, red_a, peers_a, send_a, recv_a)
 
     def rest(i, carry):
         for more in range(UNROLL):
@@ -385,11 +391,13 @@
 
     lax.fori_loop(0, NB, other_half, 0)
     for copy in first_sum:
-        copy.wait()
+        copy.wait_recv()
     part_b[...] = part_a[...] + jnp.sum(red_a[...], axis=0)
-    second_sum = exchange(part_b, red_b, peer_b, send_b, recv_b)
+    second_sum = exchange(part_b, red_b, peers_b, send_b, recv_b)
+    for copy in first_sum:
+        copy.wait_send()
     for copy in second_sum:
-        copy.wait()
+        copy.wait_recv()
     packed = part_b[...] + jnp.sum(red_b[...], axis=0)
 
     moments = jnp.concatenate([packed, turn(packed, 64)], axis=0)
@@ -423,6 +431,8 @@
             b = chunk * 4 + piece
             w_out[b] = sums[0:16, piece * OBS : (piece + 1) * OBS]
             r_out[b] = left_over[:, piece * OBS : (piece + 1) * OBS]
+    for copy in second_sum:
+        copy.wait_send()
 
 
 def on_device(innovations, ensemble, coords, obs_error, pair_cols, pair_count):

time: 36.2 us -> 35.6 us (0.983)
  Pallas kernels: 34.2 us -> 33.5 us
    pallas_call x1, Pallas kernels: 34.2 us -> 33.5 us  [on_device(): pl.pallas_call(kernel, out_shape=(out, out), in_specs=[pl.BlockSpec(memor...]
where the time goes in v3:
time: 35.6 us; the launch traced here: 35.5 us
  Pallas kernels  33.5 us (94%)
  local copies, waits for them, and re-layouts  1.31 us (4%)
  between operations  0.64 us (2%)
    pallas_call x1, Pallas kernels, on_device(): pl.pallas_call(kernel, out_shape=(out, out), in_specs=[pl.BlockSpec(memor...  33.5 us
    unnamed x2, local copies, waits for them, and re-layouts  1.31 us

profile of v3, /device:TPU:1, one launch (start us, length us, event | category | flops | bytes accessed | tf_op | source)
XLA Modules:
  0.0 35.5 jit_solution(11870990715752954203)
XLA Ops:
  0.6 33.5 %shard_map.68 = (f32[16,16,128]{2,1,0:T(8,128)S(1)}, f32[16,16,128]{2,1,0:T(8,128)S(1)}) custom-call(f32[16,16,128]{2,1,0:T(8,128)} %innov.1, f32[16,64,128]{2,1,0:T(8,128)} %ens.1, s32[16,2,128]{2,1,0:T(2,128)} %coords.1, f32[16,128]{1,0:T(8,128)} %obs.1, s32[16,9]{1,0:T(8,128)} %cols.1), custom_call_target="tpu_custom_call" | custom-call | tf_op jit(solution)/shard_map/pallas_call | solution.py:443
  34.2 0.7 %copy.9 = f32[16,16,128]{2,1,0:T(8,128)} copy(f32[16,16,128]{2,1,0:T(8,128)S(1)} %get-tuple-element.4) | data formatting | bytes 262144
  34.8 0.7 %copy.10 = f32[16,16,128]{2,1,0:T(8,128)} copy(f32[16,16,128]{2,1,0:T(8,128)S(1)} %get-tuple-element.5) | data formatting | bytes 262144

commit v4 on v3

--- a/solution.py
+++ b/solution.py
@@ -63,7 +63,7 @@
     innov, ens, coords, obs, cols, w_out, r_out,
     ens_v, crd_v, v_v, obs_v, cols_v,
     lhsx, rhs, kmat, zx, zf, maskx,
-    ens_lo, ens_hi, crd_lo, crd_hi, v_lo, v_hi, p_lo, p_hi,
+    ens_lo, ens_hi, crd_lo, crd_hi, v_lo, v_hi, p_lo, p_hi, edge_lo, edge_hi,
     part_a, part_b, red_a, red_b,
     load_sem, halo_send, halo_recv, send_a, recv_a, send_b, recv_b,
 ):
@@ -240,7 +240,11 @@
         return carry
 
     tiles(W, 0, HALF, own_mask)
-    lax.fori_loop(W + 1, 2 * W + EARLY, step, 0)
+    lax.fori_loop(W + 1, 2 * W + 1, step, 0)
+    edge_lo[...] = zf[16:32, 0 : W * OBS]
+    to_left = remote(edge_lo, p_hi, 12, left)
+    to_left.start()
+    lax.fori_loop(2 * W + 1, 2 * W + EARLY, step, 0)
     tiles(last - W, W, HALF, own_mask)
     apply_to(2 * W + EARLY - 1, HALF)
     for b in range(last - W + 1, last):
@@ -252,6 +256,10 @@
         tiles(b, 0, last + W - b, own_mask)
         apply_to(b - 1, last + W + 1 - b)
     apply_to(last + W - 1, 1)
+
+    edge_hi[...] = zf[16:32, (NB - W) * OBS : NB * OBS]
+    to_right = remote(edge_hi, p_lo, 13, right)
+    to_right.start()
 
     small[0].wait()
     small[2].wait()
@@ -265,8 +273,6 @@
         if q:
             scatter(low + 1, q, HALF, 0)
     scatter(0, W, HALF, 0)
-    to_left = remote(zf.at[16:32, 0 : W * OBS], p_hi, 12, left)
-    to_left.start()
 
     small[1].wait()
     small[3].wait()
@@ -280,8 +286,6 @@
             tiles(high - j, j, j + 1, own_mask)
     for b in range(last, last + W):
         gather(b, last + W - b, HALF, 0)
-    to_right = remote(zf.at[16:32, (NB - W) * OBS : NB * OBS], p_lo, 13, right)
-    to_right.start()
 
     tiles(2 * W + EARLY, 0, HALF, own_mask)
     lax.fori_loop(2 * W + EARLY + 1, last - W, step, 0)
@@ -336,22 +340,27 @@
     early = jnp.where(
         place == 0, of_r, jnp.where(place == 1, turn(of_p, 16), jnp.where(place == 2, of_r, turn(of_p, 16) + turn(of_h, 48)))
     )
-    across = [None] * W
-    for b in range(last, last + W):
-        start = last + W - b
-        vectors = zx[32:64, b * OBS : (b + 1) * OBS]
-        part = lax.dot_general(
-            jnp.concatenate([vectors, vectors], axis=1), kmat[b, start * OBS :, :],
-            (((1,), (1,)), ((), ())), preferred_element_type=F32,
-        )
-        part = (part[0:16] + part[16:32]) * STATIC_VAR
-        for i in range(HALF - start):
-            piece = part[:, i * OBS : (i + 1) * OBS]
-            across[i] = piece if across[i] is None else across[i] + piece
-    across = jnp.concatenate(split(jnp.concatenate(across, axis=1)), axis=0)
+    def across(row):
+        sums = [None] * W
+        for b in range(last, last + W):
+            start = last + W - b
+            vectors = zx[row : row + 32, b * OBS : (b + 1) * OBS]
+            part = lax.dot_general(
+                jnp.concatenate([vectors, vectors], axis=1), kmat[b, start * OBS :, :],
+                (((1,), (1,)), ((), ())), preferred_element_type=F32,
+            )
+            part = (part[0:16] + part[16:32]) * STATIC_VAR
+            for i in range(HALF - start):
+                piece = part[:, i * OBS : (i + 1) * OBS]
+                sums[i] = piece if sums[i] is None else sums[i] + piece
+        return jnp.concatenate(sums, axis=1)
+
+    ours = jnp.concatenate(split(across(32)), axis=0)
+    given = across(0)
     to_left.wait()
-    theirs = jnp.concatenate(split(p_hi[...]), axis=0)
-    late = product_gram(across, theirs) + product_gram(theirs, across)
+    upper_halo = p_hi[...] + given
+    theirs = jnp.concatenate(split(upper_halo), axis=0)
+    late = product_gram(ours, theirs) + product_gram(theirs, ours)
     own_part = jnp.where(place == 3, early + turn(late, 48), early)
     part_a[...] = jnp.where(lane8 < 64, own_part[0:8], turn(own_part[8:16], 64))
 
@@ -374,11 +383,19 @@
             scatter(W + i * UNROLL + more, 0, HALF, 32)
         return carry
 
-    renew(32, p_hi[...], NB + W)
+    renew(32, upper_halo, NB + W)
     for b in range(last, last + W):
         gather(b, last + W - b, HALF, 32)
     to_right.wait()
-    renew(32, p_lo[...], 0)
+    lower_halo = []
+    for b in range(W):
+        part = jnp.dot(
+            zx[0:32, W * OBS : (b + HALF) * OBS], kmat[b, (W - b) * OBS :, :], preferred_element_type=F32
+        )
+        part = part[0:16] + part[16:32]
+        part = (part[:, 0:128] + part[:, 128:256]) * STATIC_VAR
+        lower_halo.append(p_lo[:, b * OBS : (b + 1) * OBS] + part)
+    renew(32, jnp.concatenate(lower_halo, axis=1), 0)
     for b in range(W):
         scatter(b, W - b, HALF, 32)
     lax.fori_loop(0, (last - W) // UNROLL, rest, 0)
@@ -403,22 +420,35 @@
     moments = jnp.concatenate([packed, turn(packed, 64)], axis=0)
     rows = lax.broadcasted_iota(jnp.int32, (32, OBS), 0)
 
-    def column(at):
-        return jnp.broadcast_to(moments[:, at : at + 1], (16, OBS))
-
-    system = jnp.concatenate([moments, turn(moments, -32)], axis=0)
-    middle = [column(16 + j) for j in range(16)]
-    spread = [jnp.concatenate([column(32 + j), middle[j]], axis=0) for j in range(16)]
-    spread += [jnp.concatenate([middle[j], column(48 + j)], axis=0) for j in range(16)]
-    inverses = []
-    for k in range(32):
-        inverse = 1.0 / spread[k][k : k + 1, :]
-        factor = jnp.where(rows == k, 0.0, spread[k] * inverse)
-        for j in range(k + 1, 32):
-            spread[j] = spread[j] - factor * spread[j][k : k + 1, :]
-        system = system - factor * system[k : k + 1, :]
-        inverses.append(inverse)
-    system = system * jnp.concatenate(inverses, axis=0)
+    lower = turn(moments, -32)
+    system = jnp.concatenate([moments, lower], axis=0)
+    first_half = [
+        jnp.concatenate(
+            [
+                jnp.broadcast_to(moments[:, 32 + j : 33 + j], (16, OBS)),
+                jnp.broadcast_to(moments[:, 16 + j : 17 + j], (16, OBS)),
+            ],
+            axis=0,
+        )
+        for j in range(16)
+    ]
+
+    def eliminate(spread, system, base):
+        inverses = []
+        for i in range(16):
+            k = base + i
+            inverse = 1.0 / spread[i][k : k + 1, :]
+            factor = jnp.where(rows == k, 0.0, spread[i] * inverse)
+            for j in range(i + 1, 16):
+                spread[j] = spread[j] - factor * spread[j][k : k + 1, :]
+            system = system - factor * system[k : k + 1, :]
+            inverses.append(inverse)
+        scaled = system[base : base + 16] * jnp.concatenate(inverses, axis=0)
+        return jnp.concatenate([system[0:16], scaled] if base else [scaled, system[16:32]], axis=0)
+
+    system = eliminate(first_half, system, 0)
+    second_half = [jnp.broadcast_to(system[:, 16 + j : 17 + j], (32, OBS)) for j in range(16)]
+    system = eliminate(second_half, system, 16)
 
     solved = jnp.concatenate([system, jnp.zeros((96, OBS), F32)], axis=0).T
     for_w = jnp.where(lane < 32, solved[0:16, :], 0.0)
@@ -465,6 +495,8 @@
             pltpu.VMEM((W, RHS, OBS), F32),
             pltpu.VMEM((RHS, W * OBS), F32),
             pltpu.VMEM((RHS, W * OBS), F32),
+            pltpu.VMEM((RHS, W * OBS), F32),
+            pltpu.VMEM((RHS, W * OBS), F32),
             pltpu.VMEM((8, OBS), F32),
             pltpu.VMEM((8, OBS), F32),
             pltpu.VMEM((15, 8, OBS), F32),

time: 35.6 us -> 35.2 us (0.989)
  Pallas kernels: 33.5 us -> 33.1 us
    pallas_call x1, Pallas kernels: 33.5 us -> 33.1 us  [on_device(): pl.pallas_call(kernel, out_shape=(out, out), in_specs=[pl.BlockSpec(memor...]
where the time goes in v4:
time: 35.2 us; the launch traced here: 35.1 us
  Pallas kernels  33.1 us (94%)
  local copies, waits for them, and re-layouts  1.31 us (4%)
  between operations  0.64 us (2%)
    pallas_call x1, Pallas kernels, on_device(): pl.pallas_call(kernel, out_shape=(out, out), in_specs=[pl.BlockSpec(memor...  33.1 us
    unnamed x2, local copies, waits for them, and re-layouts  1.31 us

profile of v4, /device:TPU:1, one launch (start us, length us, event | category | flops | bytes accessed | tf_op | source)
XLA Modules:
  0.0 35.1 jit_solution(5404358899651137264)
XLA Ops:
  0.6 33.1 %shard_map.68 = (f32[16,16,128]{2,1,0:T(8,128)S(1)}, f32[16,16,128]{2,1,0:T(8,128)S(1)}) custom-call(f32[16,16,128]{2,1,0:T(8,128)} %innov.1, f32[16,64,128]{2,1,0:T(8,128)} %ens.1, s32[16,2,128]{2,1,0:T(2,128)} %coords.1, f32[16,128]{1,0:T(8,128)} %obs.1, s32[16,9]{1,0:T(8,128)} %cols.1), custom_call_target="tpu_custom_call" | custom-call | tf_op jit(solution)/shard_map/pallas_call | solution.py:473
  33.8 0.7 %copy.9 = f32[16,16,128]{2,1,0:T(8,128)} copy(f32[16,16,128]{2,1,0:T(8,128)S(1)} %get-tuple-element.4) | data formatting | bytes 262144
  34.4 0.7 %copy.10 = f32[16,16,128]{2,1,0:T(8,128)} copy(f32[16,16,128]{2,1,0:T(8,128)S(1)} %get-tuple-element.5) | data formatting | bytes 262144

commit v5 on v4

--- a/solution.py
+++ b/solution.py
@@ -10,7 +10,7 @@
 BF16 = jnp.bfloat16
 
 LIMIT = 40 * 1024 * 1024
-UNROLL = 4
+UNROLL = 6
 EARLY = 3
 NB = 16
 W = 4

time: 35.2 us -> 35 us (level)
  no operation moved by 1% of the time
where the time goes in v5:
time: 35 us; the launch traced here: 34.9 us
  Pallas kernels  33 us (94%)
  local copies, waits for them, and re-layouts  1.31 us (4%)
  between operations  0.64 us (2%)
    pallas_call x1, Pallas kernels, on_device(): pl.pallas_call(kernel, out_shape=(out, out), in_specs=[pl.BlockSpec(memor...  33 us
    unnamed x2, local copies, waits for them, and re-layouts  1.31 us

profile of v5, /device:TPU:1, one launch (start us, length us, event | category | flops | bytes accessed | tf_op | source)
XLA Modules:
  0.0 34.9 jit_solution(4136541073563232866)
XLA Ops:
  0.6 33.0 %shard_map.68 = (f32[16,16,128]{2,1,0:T(8,128)S(1)}, f32[16,16,128]{2,1,0:T(8,128)S(1)}) custom-call(f32[16,16,128]{2,1,0:T(8,128)} %innov.1, f32[16,64,128]{2,1,0:T(8,128)} %ens.1, s32[16,2,128]{2,1,0:T(2,128)} %coords.1, f32[16,128]{1,0:T(8,128)} %obs.1, s32[16,9]{1,0:T(8,128)} %cols.1), custom_call_target="tpu_custom_call" | custom-call | tf_op jit(solution)/shard_map/pallas_call | solution.py:473
  33.6 0.7 %copy.9 = f32[16,16,128]{2,1,0:T(8,128)} copy(f32[16,16,128]{2,1,0:T(8,128)S(1)} %get-tuple-element.4) | data formatting | bytes 262144
  34.3 0.7 %copy.10 = f32[16,16,128]{2,1,0:T(8,128)} copy(f32[16,16,128]{2,1,0:T(8,128)S(1)} %get-tuple-element.5) | data formatting | bytes 262144
